TPU v7x, 32 devices: a whole 2x2x4 slice. The times are simulated.
32 devices in a mesh: dp: 8 (over y, x, core), feat: 4 (over z).
Axes of the slice: x: 2, y: 2, z: 4, core: 2. Of those that a mesh axis runs over, the one named last changes fastest.
Arguments:
- features: bfloat16 [2048, 16384], P('dp', 'feat'), may hold values from -6 to 6
- gate: float32 [2048], P('dp'), may hold values from 0.1 to 1
- bias: float32 [16384], P('feat'), may hold values from -3 to 3
- down_weight: bfloat16 [16384, 512], P('feat', 'dp'), may hold values from -0.046875 to 0.046875
- up_weight: bfloat16 [512, 16384], P('dp', 'feat'), may hold values from -0.25 to 0.25
- cotangent: bfloat16 [2048, 16384], P(('dp', 'feat')), may hold values from -0.75 to 0.75
Outputs:
- cross_out: bfloat16 [2048, 16384], P(('dp', 'feat'))
- grad_up: float32 [512, 16384], P('dp', 'feat')
- grad_down: float32 [16384, 512], P('feat', 'dp')
- grad_bias: float32 [16384], P('feat')
- grad_in: bfloat16 [2048, 16384], P('dp', 'feat')
All inputs are finite; a program needn't handle non-finite values.
Results may differ from a plain program's by a relative error of at most 0.0049.
Values may be sent and summed in bfloat16 or wider, within the bound.
A program may use at most 128 MiB of HBM per device.

v0:
```python
import jax
import jax.numpy as jnp
from jax import lax
from jax.sharding import PartitionSpec as P


def rank_total(partial_value):
    return lax.psum(partial_value, "feat").astype(jnp.bfloat16)


def on_device(features, gate, bias, down_weight, up_weight, cotangent):
    down_full, up_full = (
        lax.all_gather(down_weight, "dp", axis=1, tiled=True),
        lax.all_gather(up_weight, "dp", axis=0, tiled=True),
    )
    low = rank_total(jnp.dot(features, down_full, preferred_element_type=jnp.float32))
    proj = jnp.dot(low, up_full, preferred_element_type=jnp.float32)
    scale = gate[:, None] * proj + bias[None, :]
    xfloat = features.astype(jnp.float32)
    cross = (xfloat * (1.0 + scale)).astype(jnp.bfloat16)
    cross_out = lax.all_to_all(cross, "feat", split_axis=0, concat_axis=1, tiled=True)
    upstream = lax.all_to_all(cotangent, "feat", split_axis=1, concat_axis=0, tiled=True).astype(
        jnp.float32
    )
    pre_grad = upstream * xfloat
    bias_terms = jnp.sum(pre_grad, axis=0)
    gated_grad = (gate[:, None] * pre_grad).astype(jnp.bfloat16)
    contract_last = (((1,), (1,)), ((), ()))
    contract_first = (((0,), (0,)), ((), ()))
    rank_grad = lax.dot_general(
        gated_grad, up_full, contract_last, preferred_element_type=jnp.float32
    )
    low_grad = rank_total(rank_grad)
    grad_up = lax.psum_scatter(
        lax.dot_general(low, gated_grad, contract_first, preferred_element_type=jnp.float32),
        "dp",
        scatter_dimension=0,
        tiled=True,
    )
    down_terms = lax.dot_general(
        features, low_grad, contract_first, preferred_element_type=jnp.float32
    )
    grad_down = lax.psum_scatter(down_terms, "dp", scatter_dimension=1, tiled=True)
    grad_bias = lax.psum(bias_terms, "dp")
    back = lax.dot_general(low_grad, down_full, contract_last, preferred_element_type=jnp.float32)
    grad_in = (upstream * (1.0 + scale) + back).astype(jnp.bfloat16)
    return (cross_out, grad_up, grad_down, grad_bias, grad_in)


def solution(mesh):
    in_specs = (
        P("dp", "feat"),
        P("dp"),
        P("feat"),
        P("feat", "dp"),
        P("dp", "feat"),
        P(("dp", "feat"), None),
    )
    out_specs = (
        P(("dp", "feat"), None),
        P("dp", "feat"),
        P("feat", "dp"),
        P("feat"),
        P("dp", "feat"),
    )
    return jax.shard_map(
        on_device, mesh=mesh, in_specs=in_specs, out_specs=out_specs, check_vma=False
    )
```

profile of v0, /device:TPU:24, one launch (start us, length us, event | category | flops | bytes accessed | tf_op | source)
XLA Modules:
  0.0 294.3 jit_solution(3887025695578284725)
XLA Ops:
  7.2 0.0 all-gather.3.cloned.1.call-start
  7.2 0.7 all-gather.3.cloned.1.call-update
  7.9 0.0 all-gather.5.cloned.1.call-start
  7.9 0.7 all-gather.5.cloned.1.call-update
  8.6 0.0 reduce-scatter.3.cloned.1.call-start
  8.7 0.0 copy-start
  8.7 0.0 copy-start.2
  8.7 1.9 copy.16
  10.6 50.8 %all_to_all.32 = bf16[64,4,4096]{2,0,1:T(8,128)(2,1)S(1)} all-to-all(bf16[64,4,4096]{2,0,1:T(8,128)(2,1)S(1)} %bitcast.33), channel_id=1, replica_groups=mesh['dp'=8,'feat'=4] {'feat'}, dimensions={1} | all-to-all | bytes 4194304 | tf_op jit(solution)/shard_map/all_to_all | solution.py:22
  61.4 0.0 copy-done
  61.4 0.0 copy-done.2
  61.4 2.2 multiply_convert_fusion
  63.6 0.0 all-gather.3.cloned.1.call-done
  63.6 4.1 %fusion.10 = f32[256,512]{1,0:T(8,128)S(1)} fusion(bf16[256,4096]{1,0:T(8,128)(2,1)} %param.6, bf16[4096,512]{0,1:T(8,128)(2,1)} %all-gather.3.cloned.1.call-done), kind=kOutput, calls=%fused_computation.18 | convolution fusion | flops 1073741824 | bytes 6815744 | tf_op jit(solution)/shard_map/dot_general | solution.py:16
  67.7 18.5 %all-gather.5.cloned.1.call-done = bf16[512,4096]{1,0:T(8,128)(2,1)} async-done(((bf16[64,4096]{1,0:T(8,128)(2,1)}), bf16[512,4096]{1,0:T(8,128)(2,1)}) %all-gather.5.cloned.1.call-update) | async-done | bytes 4194320 | tf_op jit(solution)/shard_map/all_gather | solution.py:14
  86.3 4.9 %fusion.11 = f32[256,512]{1,0:T(8,128)} fusion(bf16[256,4096]{1,0:T(8,128)(2,1)} %multiply_convert_fusion, bf16[512,4096]{1,0:T(8,128)(2,1)} %all-gather.5.cloned.1.call-done), kind=kOutput, calls=%fused_computation.19 | convolution fusion | flops 1073741824 | bytes 6815744 | tf_op jit(solution)/shard_map/dot_general | solution.py:30
  91.2 43.0 %all-reduce.2 = (bf16[256,512]{1,0:T(8,128)(2,1)S(1)}, bf16[256,512]{1,0:T(8,128)(2,1)S(1)}) all-reduce(f32[256,512]{1,0:T(8,128)S(1)} %fusion.10, f32[256,512]{1,0:T(8,128)} %fusion.11), channel_id=1, replica_groups=mesh['dp'=8,'feat'=4] {'feat'}, use_global_device_ids=true, to_apply=%region_0.0 | all-reduce | flops 262144 | bytes 1572864 | tf_op jit(solution)/shard_map/psum | solution.py:8
  134.2 6.1 %fusion.12 = f32[512,4096]{1,0:T(8,128)} fusion(bf16[256,512]{1,0:T(8,128)(2,1)S(1)} %get-tuple-element.5, bf16[256,4096]{1,0:T(8,128)(2,1)} %multiply_convert_fusion), kind=kOutput, calls=%fused_computation.20 | convolution fusion | flops 1073741824 | bytes 10747904 | tf_op jit(solution)/shard_map/dot_general | solution.py:35
  140.2 0.0 reduce-scatter.3.cloned.1.call-update
  140.3 0.0 reduce-scatter.5.cloned.1.call-start
  140.3 6.3 %convolution_bitcast_fusion = f32[4096,512]{0,1:T(8,128)} fusion(bf16[256,4096]{1,0:T(8,128)(2,1)} %param.6, bf16[256,512]{1,0:T(8,128)(2,1)S(1)} %get-tuple-element.6), kind=kOutput, calls=%fused_computation | convolution fusion | flops 1073741824 | bytes 10747904 | tf_op jit(solution)/shard_map/dot_general | solution.py:40
  146.7 0.0 copy-start.1
  146.7 0.0 reduce-scatter.5.cloned.1.call-update
  146.7 0.7 copy-done.1
  147.4 9.1 %bitcast_multiply_fusion = (f32[256,4096]{1,0:T(8,128)}, bf16[256,4096]{1,0:T(8,128)(2,1)}, f32[4096]{0:T(1024)S(1)}) fusion(bf16[64,4,4096]{2,0,1:T(8,128)(2,1)S(1)} %all_to_all.32, bf16[256,4096]{1,0:T(8,128)(2,1)} %param.6, f32[4096]{0:T(1024)S(1)} %copy-done.1, bf16[256,512]{1,0:T(8,128)(2,1)S(1)} %get-tuple-element.5, ...), kind=kOutput, calls=%fused_computation.9 | convolution fusion | flops 1084223488 | bytes 14976000 | tf_op jit(solution)/shard_map/dot_general | solution.py:17
  156.4 5.9 %all-to-all-start = ((bf16[4,64,4096]{2,1,0:T(8,128)(2,1)}), bf16[4,64,4096]{2,1,0:T(8,128)(2,1)S(1)}, u32[]{:S(2)}, u32[]{:S(2)}) async-start(bf16[4,64,4096]{2,1,0:T(8,128)(2,1)} %bitcast.31), calls=%async_computation | async-start | bytes 4194304 | tf_op jit(solution)/shard_map/all_to_all | solution.py:21
  162.3 24.2 %psum.23 = f32[4096]{0:T(1024)} all-reduce(f32[4096]{0:T(1024)S(1)} %get-tuple-element.9), channel_id=1, replica_groups=mesh['dp'=8,'feat'=4] {'dp'}, use_global_device_ids=true, to_apply=%region_5.0 | all-reduce | flops 4096 | bytes 32768 | tf_op jit(solution)/shard_map/psum | solution.py:44
  186.5 6.1 %fusion.2 = bf16[256,4096]{1,0:T(8,128)(2,1)} fusion(f32[256,4096]{1,0:T(8,128)} %get-tuple-element.7, bf16[4096,512]{0,1:T(8,128)(2,1)} %all-gather.3.cloned.1.call-done, bf16[256,512]{1,0:T(8,128)(2,1)S(1)} %get-tuple-element.6), kind=kOutput, calls=%fused_computation.7 | convolution fusion | flops 1075838976 | bytes 10747904 | tf_op jit(solution)/shard_map/dot_general | solution.py:45
  192.6 13.4 %all-to-all-done = bf16[4,64,4096]{2,1,0:T(8,128)(2,1)S(1)} async-done(((bf16[4,64,4096]{2,1,0:T(8,128)(2,1)}), bf16[4,64,4096]{2,1,0:T(8,128)(2,1)S(1)}, u32[]{:S(2)}, u32[]{:S(2)}) %all-to-all-start) | async-done | bytes 2097184 | tf_op jit(solution)/shard_map/all_to_all | solution.py:21
  206.0 1.5 copy.14
  207.4 4.7 %reduce-scatter.3.cloned.1.call-done = f32[64,4096]{1,0:T(8,128)} async-done(((f32[512,4096]{1,0:T(8,128)}), f32[64,4096]{1,0:T(8,128)}) %reduce-scatter.3.cloned.1.call-update) | async-done | bytes 1048592 | tf_op jit(solution)/shard_map/reduce_scatter | solution.py:34
  212.2 75.6 %reduce-scatter.5.cloned.1.call-done = f32[4096,64]{0,1:T(8,128)} async-done(((f32[4096,512]{0,1:T(8,128)}), f32[4096,64]{0,1:T(8,128)}) %reduce-scatter.5.cloned.1.call-update) | async-done | bytes 1048592 | tf_op jit(solution)/shard_map/reduce_scatter | solution.py:43
Async XLA Ops:
  7.2 56.5 %all-gather.3.cloned.1.call-start = ((), (), s32[]{:S(2)}) async-start(), calls=%async_computation.4 | async-start | bytes 4718592 | tf_op jit(solution)/shard_map/all_gather | solution.py:13
  7.9 78.4 %all-gather.5.cloned.1.call-start = ((), (), s32[]{:S(2)}) async-start(), calls=%async_computation.5 | async-start | bytes 4718592 | tf_op jit(solution)/shard_map/all_gather | solution.py:14
  8.6 203.5 %reduce-scatter.3.cloned.1.call-start = ((), (), s32[]{:S(2)}) async-start(), calls=%async_computation.6 | async-start | bytes 9437184 | tf_op jit(solution)/shard_map/reduce_scatter | solution.py:34
  8.7 52.7 %copy-start = (bf16[256,4096]{1,0:T(8,128)(2,1)S(1)}, bf16[256,4096]{1,0:T(8,128)(2,1)}, u32[]{:S(2)}) copy-start(bf16[256,4096]{1,0:T(8,128)(2,1)} %param.6) | copy-start | bytes 6291460
  8.7 52.7 %copy-start.2 = (f32[256]{0:T(256)S(1)}, f32[256]{0:T(256)}, u32[]{:S(2)}) copy-start(f32[256]{0:T(256)} %param.7) | copy-start | bytes 3076
  140.3 147.5 %reduce-scatter.5.cloned.1.call-start = ((), (), s32[]{:S(2)}) async-start(), calls=%async_computation.7 | async-start | bytes 9437184 | tf_op jit(solution)/shard_map/reduce_scatter | solution.py:43
  146.7 0.7 copy-start.1
  156.4 49.5 %all-to-all-start = ((bf16[4,64,4096]{2,1,0:T(8,128)(2,1)}), bf16[4,64,4096]{2,1,0:T(8,128)(2,1)S(1)}, u32[]{:S(2)}, u32[]{:S(2)}) async-start(bf16[4,64,4096]{2,1,0:T(8,128)(2,1)} %bitcast.31), calls=%async_computation | async-start | bytes 4194304 | tf_op jit(solution)/shard_map/all_to_all | solution.py:21
Sparse Core Ops, SparseCore 0:
  9.9 37.6 all-gather.2
  49.5 36.7 all-gather.4
  140.4 71.7 reduce-scatter.2
  216.4 71.2 reduce-scatter.4
where the time goes:
time: 296 us; the launch traced here: 294 us
  blocking collectives  118 us (40%)
  waiting for transfers between devices  114 us (39%)
  matrix products  36.6 us (12%)
  between operations  13.8 us (5%)
  starting transfers between devices  6.03 us (2%)
  local copies, waits for them, and re-layouts  4.03 us (1%)
    reduce_scatter x1, waiting for transfers between devices, on_device(): lax.psum_scatter(down_terms, 'dp', scatter_dimension=1, tiled=True)  75.6 us
    all_to_all x1, blocking collectives, on_device(): lax.all_to_all(cotangent, 'feat', split_axis=1, concat_axis=0, tiled=True)  50.8 us
    psum x1, blocking collectives, rank_total(): return lax.psum(partial_value, 'feat').astype(jnp.bfloat16)  43 us
    psum x1, blocking collectives, on_device(): grad_bias = lax.psum(bias_terms, 'dp')  24.2 us
    all_gather x1, waiting for transfers between devices, on_device(): lax.all_gather(up_weight, 'dp', axis=0, tiled=True)  18.5 us
    all_to_all x1, waiting for transfers between devices, on_device(): lax.all_to_all(cross, 'feat', split_axis=0, concat_axis=1, tiled=True)  13.4 us
    dot_general x1, matrix products, on_device(): proj = jnp.dot(low, up_full, preferred_element_type=jnp.float32)  9.07 us
    dot_general x1, matrix products, on_device(): lax.dot_general(features, low_grad, contract_first, preferred_element_typ...  6.34 us
  transfers between devices with their start and end apart: 5, of which 4 were waited for; matrix products, arithmetic and copies ran while one was open for 11% of the time, Pallas kernels for 0%

commit v1 on v0

--- a/solution.py
+++ b/solution.py
@@ -1,14 +1,25 @@
+import functools
+
 import jax
 import jax.numpy as jnp
 from jax import lax
+from jax.experimental import pallas as pl
+from jax.experimental.pallas import tpu as pltpu
 from jax.sharding import PartitionSpec as P
+
+MESH = pl.DeviceIdType.MESH
+F32 = jnp.float32
+BF16 = jnp.bfloat16
+NT = (((1,), (1,)), ((), ()))
+TILE = 512
+CHUNKS = 4
 
 
 def rank_total(partial_value):
     return lax.psum(partial_value, "feat").astype(jnp.bfloat16)
 
 
-def on_device(features, gate, bias, down_weight, up_weight, cotangent):
+def plain_form(features, gate, bias, down_weight, up_weight, cotangent):
     down_full, up_full = (
         lax.all_gather(down_weight, "dp", axis=1, tiled=True),
         lax.all_gather(up_weight, "dp", axis=0, tiled=True),
@@ -25,11 +36,8 @@
     pre_grad = upstream * xfloat
     bias_terms = jnp.sum(pre_grad, axis=0)
     gated_grad = (gate[:, None] * pre_grad).astype(jnp.bfloat16)
-    contract_last = (((1,), (1,)), ((), ()))
     contract_first = (((0,), (0,)), ((), ()))
-    rank_grad = lax.dot_general(
-        gated_grad, up_full, contract_last, preferred_element_type=jnp.float32
-    )
+    rank_grad = lax.dot_general(gated_grad, up_full, NT, preferred_element_type=jnp.float32)
     low_grad = rank_total(rank_grad)
     grad_up = lax.psum_scatter(
         lax.dot_general(low, gated_grad, contract_first, preferred_element_type=jnp.float32),
@@ -42,12 +50,345 @@
     )
     grad_down = lax.psum_scatter(down_terms, "dp", scatter_dimension=1, tiled=True)
     grad_bias = lax.psum(bias_terms, "dp")
-    back = lax.dot_general(low_grad, down_full, contract_last, preferred_element_type=jnp.float32)
+    back = lax.dot_general(low_grad, down_full, NT, preferred_element_type=jnp.float32)
     grad_in = (upstream * (1.0 + scale) + back).astype(jnp.bfloat16)
     return (cross_out, grad_up, grad_down, grad_bias, grad_in)
 
 
+def kernel(
+    n_dp, n_feat, steps,
+    x, cot, down, up, gate, bias,
+    cross_out, grad_up, grad_down, grad_bias, grad_in,
+    cot_v, d_full, u_full, one_scale, gated, cross,
+    acc_up, acc_down, out_up, out_down, in_up, in_down,
+    h_part, h_send, h_in, low, g_part, g_send, g_in, low_grad,
+    b_part, b_in,
+    cot_s, cot_r, ag_s, ag_r, sum_s, sum_r, all_s, all_r,
+    cross_s, cross_r, rs_s, rs_r, bias_s, bias_r, local,
+):
+    me = lax.axis_index("dp")
+    mf = lax.axis_index("feat")
+    rows, cols = x.shape
+    part = rows // n_feat
+    rank = u_full.shape[0]
+    shard = rank // n_dp
+    tiles = cols // TILE
+    odd = lax.rem(me, 2)
+
+    def flip(mask):
+        return me + mask - 2 * mask * lax.rem(lax.div(me, mask), 2)
+
+    masks = [2 ** (b + 1) for b in range(steps - 1)]
+    peers = [
+        (1 - odd) * flip(a) + odd * flip(b) for a, b in zip(masks, masks[::-1])
+    ] + [flip(1)]
+    feats = [lax.rem(mf + k, n_feat) for k in range(1, n_feat)]
+
+    def rows_of(f):
+        return pl.ds(pl.multiple_of(f * part, part), part)
+
+    def cols_of(f):
+        return pl.ds(pl.multiple_of(f * cols, cols), cols)
+
+    def tile_at(t):
+        return pl.ds(pl.multiple_of(t * TILE, TILE), TILE)
+
+    def slots(a, b):
+        return pl.ds(a * shard, (b - a) * shard)
+
+    started = []
+
+    def send(src, dst, s, r, dp, feat):
+        copy = pltpu.make_async_remote_copy(
+            src_ref=src, dst_ref=dst, send_sem=s, recv_sem=r,
+            device_id=(dp, feat), device_id_type=MESH,
+        )
+        copy.start()
+        started.append(copy)
+        return copy
+
+    def move(src, dst, s):
+        copy = pltpu.make_async_copy(src, dst, s)
+        copy.start()
+        return copy
+
+    barrier = pltpu.get_barrier_semaphore()
+    for p in peers:
+        pl.semaphore_signal(barrier, inc=1, device_id=(p, mf), device_id_type=MESH)
+    for f in feats:
+        pl.semaphore_signal(barrier, inc=1, device_id=(me, f), device_id_type=MESH)
+    pl.semaphore_wait(barrier, steps + n_feat - 1)
+
+    first = [
+        send(src, full.at[slots(1, 2), :], ag_s.at[w, 0], ag_r.at[w, 0], peers[0], mf)
+        for w, (src, full) in enumerate(((down, d_full), (up, u_full)))
+    ]
+    cot_in = [
+        send(cot.at[:, cols_of(f)], cot_v.at[rows_of(mf), :], cot_s.at[k], cot_r.at[k], me, f)
+        for k, f in enumerate(feats)
+    ]
+    own = [
+        move(down, d_full.at[slots(0, 1), :], local.at[0]),
+        move(up, u_full.at[slots(0, 1), :], local.at[1]),
+        move(cot.at[:, cols_of(mf)], cot_v.at[rows_of(mf), :], local.at[2]),
+    ]
+
+    mid = 2 ** (steps - 1)
+    half = mid // 2
+
+    def swap(w, full, s, lo, hi, to, sem):
+        return send(
+            full.at[slots(lo, hi), :], full.at[slots(to, to + hi - lo), :],
+            ag_s.at[w, sem], ag_r.at[w, sem], peers[s], mf)
+
+    hops, early = list(first), [None, None]
+    for s in range(1, steps - 1):
+        for w, full in enumerate((d_full, u_full)):
+            if s == 1:
+                own[w].wait()
+            hops[w].wait_recv()
+            hops[w] = swap(w, full, s, 0, 2 ** s, 2 ** s, s)
+            if s == steps - 2:
+                early[w] = swap(w, full, steps - 1, 0, half, mid, steps - 1)
+
+    def last_hop(w, full):
+        hops[w].wait_recv()
+        late = swap(w, full, steps - 1, half, mid, mid + half, steps)
+        early[w].wait_recv()
+        return late
+
+    def spread_parts(which, total, outgoing, incoming):
+        copies = []
+        for k, f in enumerate(feats):
+            outgoing[rows_of(f), :] = total[rows_of(f), :].astype(BF16)
+            copies.append(send(
+                outgoing.at[rows_of(f), :], incoming.at[k],
+                sum_s.at[which, k], sum_r.at[which, k], me, f))
+        return copies
+
+    def share_sum(which, total, incoming, copies, result):
+        value = total[rows_of(mf), :]
+        for k, copy in enumerate(copies):
+            copy.wait_recv()
+            value = value + incoming[k].astype(F32)
+        result[rows_of(mf), :] = value.astype(BF16)
+        return [
+            send(result.at[rows_of(mf), :], result.at[rows_of(mf), :],
+                 all_s.at[which, k], all_r.at[which, k], me, f)
+            for k, f in enumerate(feats)
+        ]
+
+    def wait_all(copies):
+        for copy in copies:
+            copy.wait_recv()
+
+    last_hop(0, d_full).wait_recv()
+    h_part[...] = jnp.zeros_like(h_part)
+
+    @pl.loop(0, tiles)
+    def _(t):
+        c = tile_at(t)
+        h_part[...] += lax.dot_general(x[:, c], d_full[:, c], NT, preferred_element_type=F32)
+
+    parts = spread_parts(0, h_part, h_send, h_in)
+    u_late = last_hop(1, u_full)
+    shares = share_sum(0, h_part, h_in, parts, low)
+    u_late.wait_recv()
+    wait_all(shares)
+
+    cross_in, own_cross = [], []
+    per_chunk = tiles // CHUNKS
+    for n in range(CHUNKS):
+
+        @pl.loop(n * per_chunk, (n + 1) * per_chunk)
+        def _(t):
+            c = tile_at(t)
+            proj = jnp.dot(low[...], u_full[:, c], preferred_element_type=F32)
+            plus = 1.0 + (gate[...] * proj + bias[:, c])
+            one_scale[:, c] = plus
+            cross[:, c] = (x[:, c].astype(F32) * plus).astype(BF16)
+
+        width = per_chunk * TILE
+        here = pl.ds(n * width, width)
+        there = pl.ds(pl.multiple_of(mf * cols + n * width, width), width)
+        for k, f in enumerate(feats):
+            cross_in.append(send(
+                cross.at[rows_of(f), here], cross_out.at[:, there],
+                cross_s.at[n, k], cross_r.at[n, k], me, f))
+        own_cross.append(move(cross.at[rows_of(mf), here], cross_out.at[:, there], local.at[3 + n]))
+
+    own[2].wait()
+    wait_all(cot_in)
+    g_part[...] = jnp.zeros_like(g_part)
+
+    @pl.loop(0, tiles)
+    def _(t):
+        c = tile_at(t)
+        pre = cot_v[:, c].astype(F32) * x[:, c].astype(F32)
+        b_part[:, c] = jnp.sum(pre.reshape(rows // 8, 8, TILE), axis=0)
+        scaled = (gate[...] * pre).astype(BF16)
+        gated[:, c] = scaled
+        g_part[...] += lax.dot_general(scaled, u_full[:, c], NT, preferred_element_type=F32)
+
+    parts = spread_parts(1, g_part, g_send, g_in)
+
+    def outer(factor, block, acc, out):
+        @pl.loop(0, tiles)
+        def _(t):
+            c = tile_at(t)
+            terms = jnp.dot(factor, block[:, c], preferred_element_type=F32)
+            acc[:, c] = terms[: mid * shard]
+            out[slots(mid, 2 * mid), c] = terms[mid * shard :].astype(BF16)
+
+    def scatter(w, s, out, arriving):
+        return send(
+            out.at[slots(2 ** s, 2 ** (s + 1)), :], arriving.at[slots(2 ** s, 2 ** (s + 1)), :],
+            rs_s.at[w, s], rs_r.at[w, s], peers[s], mf)
+
+    def fold(s, copy, acc, out, arriving, result):
+        copy.wait_recv()
+        n = 2 ** s
+
+        @pl.loop(0, tiles)
+        def _(t):
+            c = tile_at(t)
+            total = acc[slots(0, n), c] + arriving[slots(n, 2 * n), c].astype(F32)
+            if s == 0:
+                result[:, c] = total
+            else:
+                acc[slots(0, n // 2), c] = total[: n // 2 * shard]
+                out[slots(n // 2, n), c] = total[n // 2 * shard :].astype(BF16)
+
+    def bias_send(s):
+        return send(b_part, b_in.at[s], bias_s.at[s], bias_r.at[s], peers[s], mf)
+
+    def bias_fold(s, copy):
+        copy.wait()
+        started[:] = [other for other in started if other is not copy]
+        b_part[...] += b_in[s]
+
+    ups = (acc_up, out_up, in_up, grad_up)
+    downs = (acc_down, out_down, in_down, grad_down)
+    bias_hop = bias_send(steps - 1)
+    outer(low[...].astype(F32).T.astype(BF16), gated, acc_up, out_up)
+    up_hop = scatter(0, steps - 1, out_up, in_up)
+
+    shares = share_sum(1, g_part, g_in, parts, low_grad)
+    fold(steps - 1, up_hop, *ups)
+    up_hop = scatter(0, steps - 2, out_up, in_up)
+    wait_all(shares)
+
+    outer(low_grad[...].astype(F32).T.astype(BF16), x, acc_down, out_down)
+    down_hop = scatter(1, steps - 1, out_down, in_down)
+    bias_fold(steps - 1, bias_hop)
+    bias_hop = bias_send(steps - 2)
+    fold(steps - 1, down_hop, *downs)
+    down_hop = scatter(1, steps - 2, out_down, in_down)
+
+    @pl.loop(0, tiles)
+    def _(t):
+        c = tile_at(t)
+        back = jnp.dot(low_grad[...], d_full[:, c], preferred_element_type=F32)
+        grad_in[:, c] = (cot_v[:, c].astype(F32) * one_scale[:, c] + back).astype(BF16)
+
+    for s in range(steps - 2, -1, -1):
+        fold(s, up_hop, *ups)
+        if s:
+            up_hop = scatter(0, s - 1, out_up, in_up)
+        fold(s, down_hop, *downs)
+        if s:
+            down_hop = scatter(1, s - 1, out_down, in_down)
+        bias_fold(s, bias_hop)
+        if s:
+            bias_hop = bias_send(s - 1)
+    grad_bias[...] = jnp.sum(b_part[...], axis=0, keepdims=True)
+
+    wait_all(cross_in)
+    for copy in own_cross:
+        copy.wait()
+    for copy in started:
+        copy.wait_send()
+
+
+def kernel_form(n_dp, n_feat, features, gate, bias, down_weight, up_weight, cotangent):
+    rows, cols = features.shape
+    shard = up_weight.shape[0]
+    rank = shard * n_dp
+    part = rows // n_feat
+    steps = n_dp.bit_length() - 1
+    vmem = pl.BlockSpec(memory_space=pltpu.VMEM)
+    hbm = pl.BlockSpec(memory_space=pl.ANY)
+    dma = pltpu.SemaphoreType.DMA
+    others = n_feat - 1
+    cross_out, grad_up, grad_down, grad_bias, grad_in = pl.pallas_call(
+        functools.partial(kernel, n_dp, n_feat, steps),
+        out_shape=(
+            jax.ShapeDtypeStruct((part, cols * n_feat), BF16),
+            jax.ShapeDtypeStruct((shard, cols), F32),
+            jax.ShapeDtypeStruct((shard, cols), F32),
+            jax.ShapeDtypeStruct((1, cols), F32),
+            jax.ShapeDtypeStruct((rows, cols), BF16),
+        ),
+        in_specs=[vmem, hbm, hbm, hbm, vmem, vmem],
+        out_specs=(hbm, vmem, vmem, vmem, vmem),
+        scratch_shapes=[
+            pltpu.VMEM((rows, cols), BF16),
+            pltpu.VMEM((rank, cols), BF16),
+            pltpu.VMEM((rank, cols), BF16),
+            pltpu.VMEM((rows, cols), F32),
+            pltpu.VMEM((rows, cols), BF16),
+            pltpu.VMEM((rows, cols), BF16),
+            pltpu.VMEM((rank // 2, cols), F32),
+            pltpu.VMEM((rank // 2, cols), F32),
+            pltpu.VMEM((rank, cols), BF16),
+            pltpu.VMEM((rank, cols), BF16),
+            pltpu.VMEM((rank, cols), BF16),
+            pltpu.VMEM((rank, cols), BF16),
+            pltpu.VMEM((rows, rank), F32),
+            pltpu.VMEM((rows, rank), BF16),
+            pltpu.VMEM((others, part, rank), BF16),
+            pltpu.VMEM((rows, rank), BF16),
+            pltpu.VMEM((rows, rank), F32),
+            pltpu.VMEM((rows, rank), BF16),
+            pltpu.VMEM((others, part, rank), BF16),
+            pltpu.VMEM((rows, rank), BF16),
+            pltpu.VMEM((8, cols), F32),
+            pltpu.VMEM((steps, 8, cols), F32),
+            dma((others,)), dma((others,)),
+            dma((2, steps + 1)), dma((2, steps + 1)),
+            dma((2, others)), dma((2, others)),
+            dma((2, others)), dma((2, others)),
+            dma((CHUNKS, others)), dma((CHUNKS, others)),
+            dma((2, steps)), dma((2, steps)),
+            dma((steps,)), dma((steps,)),
+            dma((3 + CHUNKS,)),
+        ],
+        compiler_params=pltpu.CompilerParams(
+            collective_id=0, has_side_effects=True, vmem_limit_bytes=62 * 2 ** 20
+        ),
+        cost_estimate=pl.CostEstimate(
+            flops=12 * rows * rank * cols, bytes_accessed=16 * rows * cols, transcendentals=0
+        ),
+    )(features, cotangent, down_weight.T, up_weight, gate[:, None], bias[None, :])
+    return cross_out, grad_up, grad_down.T, grad_bias[0], grad_in
+
+
 def solution(mesh):
+    n_dp, n_feat = mesh.shape["dp"], mesh.shape["feat"]
+
+    def on_device(features, gate, bias, down_weight, up_weight, cotangent):
+        rows, cols = features.shape
+        fits = (
+            n_dp >= 4
+            and n_dp & (n_dp - 1) == 0
+            and n_feat > 1
+            and up_weight.shape[0] % 16 == 0
+            and rows % (16 * n_feat) == 0
+            and cols % (TILE * CHUNKS) == 0
+        )
+        args = (features, gate, bias, down_weight, up_weight, cotangent)
+        return kernel_form(n_dp, n_feat, *args) if fits else plain_form(*args)
+
     in_specs = (
         P("dp", "feat"),
         P("dp"),

time: 296 us -> 172 us (0.58)
  Pallas kernels: 0 us -> 162 us
  blocking collectives: 118 us -> 0 us
  waiting for transfers between devices: 114 us -> 0 us
  matrix products: 36.6 us -> 0 us
  between operations: 13.8 us -> 0.66 us
  starting transfers between devices: 6.03 us -> 0 us
  local copies, waits for them, and re-layouts: 4.03 us -> 8.55 us
    pallas_call x0 -> x1, Pallas kernels: none -> 162 us  [kernel_form(): pl.pallas_call(functools.partial(kernel, n_dp, n_feat, steps), out_shape=...]
    reduce_scatter x2 -> x0, waiting for transfers between devices: 80.3 us -> none  [the longest x1 75.6 us: on_device(): lax.psum_scatter(down_terms, 'dp', scatter_dimension=1, tiled=True)]
    psum x2 -> x0, blocking collectives: 67.2 us -> none  [the longest x1 43 us: rank_total(): return lax.psum(partial_value, 'feat').astype(jnp.bfloat16)]
    all_to_all x1 -> x0, blocking collectives: 50.8 us -> none  [on_device(): lax.all_to_all(cotangent, 'feat', split_axis=1, concat_axis=0, tiled=True)]
    dot_general x6 -> x0, matrix products: 36.6 us -> none  [the longest x1 9.07 us: on_device(): proj = jnp.dot(low, up_full, preferred_element_type=jnp.float32)]
    all_gather x2 -> x0, waiting for transfers between devices: 18.5 us -> none  [the longest x1 18.5 us: on_device(): lax.all_gather(up_weight, 'dp', axis=0, tiled=True)]
    all_to_all x1 -> x0, waiting for transfers between devices: 13.4 us -> none  [on_device(): lax.all_to_all(cross, 'feat', split_axis=0, concat_axis=1, tiled=True)]
    unnamed x6 -> x13, local copies, waits for them, and re-layouts: 0.7 us -> 7.07 us
  transfers between devices with their start and end apart: 5 -> 0, of which waited for: 4 -> 0; matrix products, arithmetic and copies ran while one was open for 11% -> 0% of each run, Pallas kernels for 0% -> 0%
where the time goes in v1:
time: 172 us; the launch traced here: 171 us
  Pallas kernels  162 us (94%)
  local copies, waits for them, and re-layouts  8.55 us (5%)
    pallas_call x1, Pallas kernels, kernel_form(): pl.pallas_call(functools.partial(kernel, n_dp, n_feat, steps), out_shape=...  162 us
    unnamed x13, local copies, waits for them, and re-layouts  7.07 us

profile of v1, /device:TPU:24, one launch (start us, length us, event | category | flops | bytes accessed | tf_op | source)
XLA Modules:
  0.0 171.4 jit_solution(10199249042813208767)
XLA Ops:
  0.6 1.5 copy.11.gate
  2.1 162.2 %shard_map.101 = (bf16[64,16384]{1,0:T(8,128)(2,1)}, f32[64,4096]{1,0:T(8,128)}, f32[64,4096]{1,0:T(8,128)}, f32[1,4096]{1,0:T(1,128)}, bf16[256,4096]{1,0:T(8,128)(2,1)}) custom-call(bf16[256,4096]{1,0:T(8,128)(2,1)} %x.1, bf16[64,16384]{1,0:T(8,128)(2,1)} %cot.1, bf16[64,4096]{1,0:T(8,128)(2,1)} %bitcast.8, bf16[64,4096]{1,0:T(8,128)(2,1)} %up.1, ...), custom_call_target="tpu_custom_call" | custom-call | flops 6442450944 | bytes 16777216 | tf_op jit(solution)/shard_map/pallas_call | solution.py:323
  164.3 0.0 copy-start.2
  164.3 0.0 copy-start.1
  164.4 3.2 %copy.17 = bf16[64,16384]{1,0:T(8,128)(2,1)} copy(bf16[64,16384]{1,0:T(8,128)(2,1)} %get-tuple-element.20) | data formatting | bytes 4194304
  167.5 0.0 copy-done.2
  167.5 0.0 copy-start.3
  167.6 0.0 copy-start
  167.6 1.0 copy.18
  168.5 0.0 copy-done.1
  168.5 1.0 copy.19
  169.5 0.0 copy-done.3
  169.5 0.6 copy.20
  170.1 0.0 copy-done
  170.1 1.3 copy.21
Async XLA Ops:
  164.3 3.2 %copy-start.2 = (f32[64,4096]{1,0:T(8,128)S(1)}, f32[64,4096]{1,0:T(8,128)}, u32[]{:S(2)}) copy-start(f32[64,4096]{1,0:T(8,128)} %get-tuple-element.21) | copy-start | bytes 3145732
  164.3 4.2 %copy-start.1 = (f32[64,4096]{1,0:T(8,128)S(1)}, f32[64,4096]{1,0:T(8,128)}, u32[]{:S(2)}) copy-start(f32[64,4096]{1,0:T(8,128)} %get-tuple-element.12) | copy-start | bytes 3145732
  167.5 1.9 %copy-start.3 = (f32[1,4096]{1,0:T(1,128)S(1)}, f32[1,4096]{1,0:T(1,128)}, u32[]{:S(2)}) copy-start(f32[1,4096]{1,0:T(1,128)} %get-tuple-element.13) | copy-start | bytes 49156
  167.6 2.6 %copy-start = (bf16[256,4096]{1,0:T(8,128)(2,1)S(1)}, bf16[256,4096]{1,0:T(8,128)(2,1)}, u32[]{:S(2)}) copy-start(bf16[256,4096]{1,0:T(8,128)(2,1)} %get-tuple-element.24) | copy-start | bytes 6291460

commit v2 on v1

--- a/solution.py
+++ b/solution.py
@@ -12,7 +12,6 @@
 BF16 = jnp.bfloat16
 NT = (((1,), (1,)), ((), ()))
 TILE = 512
-CHUNKS = 4
 
 
 def rank_total(partial_value):
@@ -59,9 +58,9 @@
     n_dp, n_feat, steps,
     x, cot, down, up, gate, bias,
     cross_out, grad_up, grad_down, grad_bias, grad_in,
-    cot_v, d_full, u_full, one_scale, gated, cross,
-    acc_up, acc_down, out_up, out_down, in_up, in_down,
-    h_part, h_send, h_in, low, g_part, g_send, g_in, low_grad,
+    cot_v, d_full, u_full, one_scale, cross,
+    low_t, acc_up, acc_down, out_up, out_down, in_up, in_down,
+    gate_v, h_part, h_send, h_in, low, g_part, g_send, g_in, low_grad,
     b_part, b_in,
     cot_s, cot_r, ag_s, ag_r, sum_s, sum_r, all_s, all_r,
     cross_s, cross_r, rs_s, rs_r, bias_s, bias_r, local,
@@ -112,26 +111,40 @@
         copy.start()
         return copy
 
+    def cot_copy(t, k, f):
+        there = pl.ds(pl.multiple_of(f * cols + t * TILE, TILE), TILE)
+        return pltpu.make_async_remote_copy(
+            src_ref=cot.at[:, there], dst_ref=cot_v.at[rows_of(mf), tile_at(t)],
+            send_sem=cot_s.at[t, k], recv_sem=cot_r.at[t, k],
+            device_id=(me, f), device_id_type=MESH,
+        )
+
+    def cross_copy(t, k, f):
+        there = pl.ds(pl.multiple_of(mf * cols + t * TILE, TILE), TILE)
+        return pltpu.make_async_remote_copy(
+            src_ref=cross.at[rows_of(f), tile_at(t)], dst_ref=cross_out.at[:, there],
+            send_sem=cross_s.at[t, k], recv_sem=cross_r.at[t, k],
+            device_id=(me, f), device_id_type=MESH,
+        )
+
+    def start_chunks(copy_of, lo, hi):
+        @pl.loop(lo, hi)
+        def _(t):
+            for k, f in enumerate(feats):
+                copy_of(t, k, f).start()
+
     barrier = pltpu.get_barrier_semaphore()
     for p in peers:
         pl.semaphore_signal(barrier, inc=1, device_id=(p, mf), device_id_type=MESH)
     for f in feats:
         pl.semaphore_signal(barrier, inc=1, device_id=(me, f), device_id_type=MESH)
-    pl.semaphore_wait(barrier, steps + n_feat - 1)
-
-    first = [
-        send(src, full.at[slots(1, 2), :], ag_s.at[w, 0], ag_r.at[w, 0], peers[0], mf)
-        for w, (src, full) in enumerate(((down, d_full), (up, u_full)))
-    ]
-    cot_in = [
-        send(cot.at[:, cols_of(f)], cot_v.at[rows_of(mf), :], cot_s.at[k], cot_r.at[k], me, f)
-        for k, f in enumerate(feats)
-    ]
     own = [
         move(down, d_full.at[slots(0, 1), :], local.at[0]),
         move(up, u_full.at[slots(0, 1), :], local.at[1]),
         move(cot.at[:, cols_of(mf)], cot_v.at[rows_of(mf), :], local.at[2]),
     ]
+    gate_v[...] = jnp.broadcast_to(gate[...], (128, rows)).T
+    pl.semaphore_wait(barrier, steps + n_feat - 1)
 
     mid = 2 ** (steps - 1)
     half = mid // 2
@@ -141,21 +154,23 @@
             full.at[slots(lo, hi), :], full.at[slots(to, to + hi - lo), :],
             ag_s.at[w, sem], ag_r.at[w, sem], peers[s], mf)
 
-    hops, early = list(first), [None, None]
-    for s in range(1, steps - 1):
-        for w, full in enumerate((d_full, u_full)):
-            if s == 1:
-                own[w].wait()
-            hops[w].wait_recv()
-            hops[w] = swap(w, full, s, 0, 2 ** s, 2 ** s, s)
+    early = [None, None]
+
+    def first_hop(w, src, full):
+        return send(src, full.at[slots(1, 2), :], ag_s.at[w, 0], ag_r.at[w, 0], peers[0], mf)
+
+    def middle_hops(w, full, hop):
+        own[w].wait()
+        for s in range(1, steps - 1):
+            hop.wait_recv()
+            hop = swap(w, full, s, 0, 2 ** s, 2 ** s, s)
             if s == steps - 2:
                 early[w] = swap(w, full, steps - 1, 0, half, mid, steps - 1)
-
-    def last_hop(w, full):
-        hops[w].wait_recv()
-        late = swap(w, full, steps - 1, half, mid, mid + half, steps)
-        early[w].wait_recv()
-        return late
+        return hop
+
+    def last_hop(w, full, hop):
+        hop.wait_recv()
+        return swap(w, full, steps - 1, half, mid, mid + half, steps)
 
     def spread_parts(which, total, outgoing, incoming):
         copies = []
@@ -182,63 +197,64 @@
         for copy in copies:
             copy.wait_recv()
 
-    last_hop(0, d_full).wait_recv()
-    h_part[...] = jnp.zeros_like(h_part)
+    def bias_send(s):
+        return send(b_part, b_in.at[s], bias_s.at[s], bias_r.at[s], peers[s], mf)
+
+    def bias_fold(s, copy):
+        copy.wait()
+        started[:] = [other for other in started if other is not copy]
+        b_part[...] += b_in[s]
+
+    hop = first_hop(0, down, d_full)
+    start_chunks(cot_copy, 0, tiles // 2)
+    hop = middle_hops(0, d_full, hop)
+    late = last_hop(0, d_full, hop)
+    hop = first_hop(1, up, u_full)
+    near, far = slots(0, mid), slots(mid, 2 * mid)
+    h_part[:, near] = lax.dot_general(x[...], d_full[near, :], NT, preferred_element_type=F32)
+    early[0].wait_recv()
+    late.wait_recv()
+    h_part[:, far] = lax.dot_general(x[...], d_full[far, :], NT, preferred_element_type=F32)
+    parts = spread_parts(0, h_part, h_send, h_in)
+    start_chunks(cot_copy, tiles // 2, tiles // 2 + 1)
+    hop = middle_hops(1, u_full, hop)
+    shares = share_sum(0, h_part, h_in, parts, low)
+    start_chunks(cot_copy, tiles // 2 + 1, tiles)
+    late = last_hop(1, u_full, hop)
+    wait_all(shares)
+    early[1].wait_recv()
+    late.wait_recv()
 
     @pl.loop(0, tiles)
     def _(t):
         c = tile_at(t)
-        h_part[...] += lax.dot_general(x[:, c], d_full[:, c], NT, preferred_element_type=F32)
-
-    parts = spread_parts(0, h_part, h_send, h_in)
-    u_late = last_hop(1, u_full)
-    shares = share_sum(0, h_part, h_in, parts, low)
-    u_late.wait_recv()
-    wait_all(shares)
-
-    cross_in, own_cross = [], []
-    per_chunk = tiles // CHUNKS
-    for n in range(CHUNKS):
-
-        @pl.loop(n * per_chunk, (n + 1) * per_chunk)
-        def _(t):
-            c = tile_at(t)
-            proj = jnp.dot(low[...], u_full[:, c], preferred_element_type=F32)
-            plus = 1.0 + (gate[...] * proj + bias[:, c])
-            one_scale[:, c] = plus
-            cross[:, c] = (x[:, c].astype(F32) * plus).astype(BF16)
-
-        width = per_chunk * TILE
-        here = pl.ds(n * width, width)
-        there = pl.ds(pl.multiple_of(mf * cols + n * width, width), width)
-        for k, f in enumerate(feats):
-            cross_in.append(send(
-                cross.at[rows_of(f), here], cross_out.at[:, there],
-                cross_s.at[n, k], cross_r.at[n, k], me, f))
-        own_cross.append(move(cross.at[rows_of(mf), here], cross_out.at[:, there], local.at[3 + n]))
+        proj = jnp.dot(low[...], u_full[:, c], preferred_element_type=F32)
+        plus = 1.0 + (gate_v[:, :1] * proj + bias[:, c])
+        one_scale[:, c] = plus
+        cross[:, c] = (x[:, c].astype(F32) * plus).astype(BF16)
+
+    start_chunks(cross_copy, 0, tiles // 4)
+    own_cross = move(cross.at[rows_of(mf), :], cross_out.at[:, cols_of(mf)], local.at[3])
 
     own[2].wait()
-    wait_all(cot_in)
     g_part[...] = jnp.zeros_like(g_part)
+    low_t[...] = low[...].astype(F32).T.astype(BF16)
 
     @pl.loop(0, tiles)
     def _(t):
         c = tile_at(t)
+        for k, f in enumerate(feats):
+            cot_copy(t, k, f).wait_recv()
         pre = cot_v[:, c].astype(F32) * x[:, c].astype(F32)
         b_part[:, c] = jnp.sum(pre.reshape(rows // 8, 8, TILE), axis=0)
-        scaled = (gate[...] * pre).astype(BF16)
-        gated[:, c] = scaled
+        scaled = (gate_v[:, :1] * pre).astype(BF16)
         g_part[...] += lax.dot_general(scaled, u_full[:, c], NT, preferred_element_type=F32)
+        terms = jnp.dot(low_t[...], scaled, preferred_element_type=F32)
+        acc_up[:, c] = terms[: mid * shard]
+        out_up[far, c] = terms[mid * shard :].astype(BF16)
 
     parts = spread_parts(1, g_part, g_send, g_in)
-
-    def outer(factor, block, acc, out):
-        @pl.loop(0, tiles)
-        def _(t):
-            c = tile_at(t)
-            terms = jnp.dot(factor, block[:, c], preferred_element_type=F32)
-            acc[:, c] = terms[: mid * shard]
-            out[slots(mid, 2 * mid), c] = terms[mid * shard :].astype(BF16)
+    start_chunks(cross_copy, tiles // 4, tiles // 2)
 
     def scatter(w, s, out, arriving):
         return send(
@@ -259,26 +275,25 @@
                 acc[slots(0, n // 2), c] = total[: n // 2 * shard]
                 out[slots(n // 2, n), c] = total[n // 2 * shard :].astype(BF16)
 
-    def bias_send(s):
-        return send(b_part, b_in.at[s], bias_s.at[s], bias_r.at[s], peers[s], mf)
-
-    def bias_fold(s, copy):
-        copy.wait()
-        started[:] = [other for other in started if other is not copy]
-        b_part[...] += b_in[s]
-
     ups = (acc_up, out_up, in_up, grad_up)
     downs = (acc_down, out_down, in_down, grad_down)
     bias_hop = bias_send(steps - 1)
-    outer(low[...].astype(F32).T.astype(BF16), gated, acc_up, out_up)
     up_hop = scatter(0, steps - 1, out_up, in_up)
 
     shares = share_sum(1, g_part, g_in, parts, low_grad)
+    start_chunks(cross_copy, tiles // 2, tiles)
     fold(steps - 1, up_hop, *ups)
     up_hop = scatter(0, steps - 2, out_up, in_up)
     wait_all(shares)
-
-    outer(low_grad[...].astype(F32).T.astype(BF16), x, acc_down, out_down)
+    low_t[...] = low_grad[...].astype(F32).T.astype(BF16)
+
+    @pl.loop(0, tiles)
+    def _(t):
+        c = tile_at(t)
+        terms = jnp.dot(low_t[...], x[:, c], preferred_element_type=F32)
+        acc_down[:, c] = terms[: mid * shard]
+        out_down[far, c] = terms[mid * shard :].astype(BF16)
+
     down_hop = scatter(1, steps - 1, out_down, in_down)
     bias_fold(steps - 1, bias_hop)
     bias_hop = bias_send(steps - 2)
@@ -303,9 +318,14 @@
             bias_hop = bias_send(s - 1)
     grad_bias[...] = jnp.sum(b_part[...], axis=0, keepdims=True)
 
-    wait_all(cross_in)
-    for copy in own_cross:
-        copy.wait()
+    @pl.loop(0, tiles)
+    def _(t):
+        for k, f in enumerate(feats):
+            cross_copy(t, k, f).wait_recv()
+            cross_copy(t, k, f).wait_send()
+            cot_copy(t, k, f).wait_send()
+
+    own_cross.wait()
     for copy in started:
         copy.wait_send()
 
@@ -320,6 +340,7 @@
     hbm = pl.BlockSpec(memory_space=pl.ANY)
     dma = pltpu.SemaphoreType.DMA
     others = n_feat - 1
+    tiles = cols // TILE
     cross_out, grad_up, grad_down, grad_bias, grad_in = pl.pallas_call(
         functools.partial(kernel, n_dp, n_feat, steps),
         out_shape=(
@@ -337,13 +358,14 @@
             pltpu.VMEM((rank, cols), BF16),
             pltpu.VMEM((rows, cols), F32),
             pltpu.VMEM((rows, cols), BF16),
-            pltpu.VMEM((rows, cols), BF16),
+            pltpu.VMEM((rank, rows), BF16),
             pltpu.VMEM((rank // 2, cols), F32),
             pltpu.VMEM((rank // 2, cols), F32),
             pltpu.VMEM((rank, cols), BF16),
             pltpu.VMEM((rank, cols), BF16),
             pltpu.VMEM((rank, cols), BF16),
             pltpu.VMEM((rank, cols), BF16),
+            pltpu.VMEM((rows, 128), F32),
             pltpu.VMEM((rows, rank), F32),
             pltpu.VMEM((rows, rank), BF16),
             pltpu.VMEM((others, part, rank), BF16),
@@ -354,14 +376,14 @@
             pltpu.VMEM((rows, rank), BF16),
             pltpu.VMEM((8, cols), F32),
             pltpu.VMEM((steps, 8, cols), F32),
-            dma((others,)), dma((others,)),
+            dma((tiles, others)), dma((tiles, others)),
             dma((2, steps + 1)), dma((2, steps + 1)),
             dma((2, others)), dma((2, others)),
             dma((2, others)), dma((2, others)),
-            dma((CHUNKS, others)), dma((CHUNKS, others)),
+            dma((tiles, others)), dma((tiles, others)),
             dma((2, steps)), dma((2, steps)),
             dma((steps,)), dma((steps,)),
-            dma((3 + CHUNKS,)),
+            dma((4,)),
         ],
         compiler_params=pltpu.CompilerParams(
             collective_id=0, has_side_effects=True, vmem_limit_bytes=62 * 2 ** 20
@@ -369,7 +391,7 @@
         cost_estimate=pl.CostEstimate(
             flops=12 * rows * rank * cols, bytes_accessed=16 * rows * cols, transcendentals=0
         ),
-    )(features, cotangent, down_weight.T, up_weight, gate[:, None], bias[None, :])
+    )(features, cotangent, down_weight.T, up_weight, gate[None, :], bias[None, :])
     return cross_out, grad_up, grad_down.T, grad_bias[0], grad_in
 
 
@@ -384,7 +406,7 @@
             and n_feat > 1
             and up_weight.shape[0] % 16 == 0
             and rows % (16 * n_feat) == 0
-            and cols % (TILE * CHUNKS) == 0
+            and cols % TILE == 0 and cols // TILE >= 8
         )
         args = (features, gate, bias, down_weight, up_weight, cotangent)
         return kernel_form(n_dp, n_feat, *args) if fits else plain_form(*args)

time: 172 us -> 160 us (0.930); the launches traced: 171 us -> 157 us
  Pallas kernels: 162 us -> 149 us
    pallas_call x1, Pallas kernels: 162 us -> 149 us  [kernel_form(): pl.pallas_call(functools.partial(kernel, n_dp, n_feat, steps), out_shape=...]
where the time goes in v2:
time: 160 us; the launch traced here: 157 us
  Pallas kernels  149 us (93%)
  local copies, waits for them, and re-layouts  7.07 us (4%)
    pallas_call x1, Pallas kernels, kernel_form(): pl.pallas_call(functools.partial(kernel, n_dp, n_feat, steps), out_shape=...  149 us
    unnamed x13, local copies, waits for them, and re-layouts  7.07 us

profile of v2, /device:TPU:24, one launch (start us, length us, event | category | flops | bytes accessed | tf_op | source)
XLA Modules:
  0.0 157.1 jit_solution(4549193441663552118)
XLA Ops:
  0.6 149.3 %shard_map.101 = (bf16[64,16384]{1,0:T(8,128)(2,1)}, f32[64,4096]{1,0:T(8,128)}, f32[64,4096]{1,0:T(8,128)}, f32[1,4096]{1,0:T(1,128)}, bf16[256,4096]{1,0:T(8,128)(2,1)}) custom-call(bf16[256,4096]{1,0:T(8,128)(2,1)} %x.1, bf16[64,16384]{1,0:T(8,128)(2,1)} %cot.1, bf16[64,4096]{1,0:T(8,128)(2,1)} %bitcast.7, bf16[64,4096]{1,0:T(8,128)(2,1)} %up.1, ...), custom_call_target="tpu_custom_call" | custom-call | flops 6442450944 | bytes 16777216 | tf_op jit(solution)/shard_map/pallas_call | solution.py:344
  150.0 0.0 copy-start.2
  150.0 0.0 copy-start.1
  150.0 3.2 %copy.16 = bf16[64,16384]{1,0:T(8,128)(2,1)} copy(bf16[64,16384]{1,0:T(8,128)(2,1)} %get-tuple-element.20) | data formatting | bytes 4194304
  153.2 0.0 copy-done.2
  153.2 0.0 copy-start.3
  153.2 0.0 copy-start
  153.2 1.0 copy.17
  154.2 0.0 copy-done.1
  154.2 1.0 copy.18
  155.1 0.0 copy-done.3
  155.1 0.6 copy.19
  155.7 0.0 copy-done
  155.7 1.3 copy.20
Async XLA Ops:
  150.0 3.2 %copy-start.2 = (f32[64,4096]{1,0:T(8,128)S(1)}, f32[64,4096]{1,0:T(8,128)}, u32[]{:S(2)}) copy-start(f32[64,4096]{1,0:T(8,128)} %get-tuple-element.21) | copy-start | bytes 3145732
  150.0 4.2 %copy-start.1 = (f32[64,4096]{1,0:T(8,128)S(1)}, f32[64,4096]{1,0:T(8,128)}, u32[]{:S(2)}) copy-start(f32[64,4096]{1,0:T(8,128)} %get-tuple-element.12) | copy-start | bytes 3145732
  153.2 1.9 %copy-start.3 = (f32[1,4096]{1,0:T(1,128)S(1)}, f32[1,4096]{1,0:T(1,128)}, u32[]{:S(2)}) copy-start(f32[1,4096]{1,0:T(1,128)} %get-tuple-element.13) | copy-start | bytes 49156
  153.2 2.6 %copy-start = (bf16[256,4096]{1,0:T(8,128)(2,1)S(1)}, bf16[256,4096]{1,0:T(8,128)(2,1)}, u32[]{:S(2)}) copy-start(bf16[256,4096]{1,0:T(8,128)(2,1)} %get-tuple-element.24) | copy-start | bytes 6291460

commit v3 on v2

--- a/solution.py
+++ b/solution.py
@@ -206,7 +206,7 @@
         b_part[...] += b_in[s]
 
     hop = first_hop(0, down, d_full)
-    start_chunks(cot_copy, 0, tiles // 2)
+    start_chunks(cot_copy, 0, tiles * 3 // 4)
     hop = middle_hops(0, d_full, hop)
     late = last_hop(0, d_full, hop)
     hop = first_hop(1, up, u_full)
@@ -216,10 +216,10 @@
     late.wait_recv()
     h_part[:, far] = lax.dot_general(x[...], d_full[far, :], NT, preferred_element_type=F32)
     parts = spread_parts(0, h_part, h_send, h_in)
-    start_chunks(cot_copy, tiles // 2, tiles // 2 + 1)
+    start_chunks(cot_copy, tiles * 3 // 4, tiles * 7 // 8)
     hop = middle_hops(1, u_full, hop)
     shares = share_sum(0, h_part, h_in, parts, low)
-    start_chunks(cot_copy, tiles // 2 + 1, tiles)
+    start_chunks(cot_copy, tiles * 7 // 8, tiles)
     late = last_hop(1, u_full, hop)
     wait_all(shares)
     early[1].wait_recv()
@@ -233,7 +233,7 @@
         one_scale[:, c] = plus
         cross[:, c] = (x[:, c].astype(F32) * plus).astype(BF16)
 
-    start_chunks(cross_copy, 0, tiles // 4)
+    start_chunks(cross_copy, 0, tiles * 3 // 8)
     own_cross = move(cross.at[rows_of(mf), :], cross_out.at[:, cols_of(mf)], local.at[3])
 
     own[2].wait()
@@ -254,7 +254,7 @@
         out_up[far, c] = terms[mid * shard :].astype(BF16)
 
     parts = spread_parts(1, g_part, g_send, g_in)
-    start_chunks(cross_copy, tiles // 4, tiles // 2)
+    start_chunks(cross_copy, tiles * 3 // 8, tiles * 5 // 8)
 
     def scatter(w, s, out, arriving):
         return send(
@@ -281,7 +281,7 @@
     up_hop = scatter(0, steps - 1, out_up, in_up)
 
     shares = share_sum(1, g_part, g_in, parts, low_grad)
-    start_chunks(cross_copy, tiles // 2, tiles)
+    start_chunks(cross_copy, tiles * 5 // 8, tiles)
     fold(steps - 1, up_hop, *ups)
     up_hop = scatter(0, steps - 2, out_up, in_up)
     wait_all(shares)
@@ -330,6 +330,34 @@
         copy.wait_send()
 
 
+def hand_over(*refs):
+    count = len(refs) // 2
+    sems = refs[-1]
+    copies = []
+    for src, dst in zip(refs[:count], refs[count:-1]):
+        rows = src.shape[0]
+        pieces = 4 if rows % 64 == 0 else 1
+        for n in range(pieces):
+            at = pl.ds(n * (rows // pieces), rows // pieces)
+            copy = pltpu.make_async_copy(src.at[at, :], dst.at[at, :], sems.at[len(copies)])
+            copy.start()
+            copies.append(copy)
+    for copy in copies:
+        copy.wait()
+
+
+def placed(*values):
+    anywhere = [pl.BlockSpec(memory_space=pl.ANY)] * len(values)
+    return pl.pallas_call(
+        hand_over,
+        out_shape=tuple(jax.ShapeDtypeStruct(v.shape, v.dtype) for v in values),
+        in_specs=anywhere,
+        out_specs=tuple(anywhere),
+        scratch_shapes=[pltpu.SemaphoreType.DMA((4 * len(values),))],
+        compiler_params=pltpu.CompilerParams(vmem_limit_bytes=62 * 2 ** 20),
+    )(*values)
+
+
 def kernel_form(n_dp, n_feat, features, gate, bias, down_weight, up_weight, cotangent):
     rows, cols = features.shape
     shard = up_weight.shape[0]
@@ -341,7 +369,7 @@
     dma = pltpu.SemaphoreType.DMA
     others = n_feat - 1
     tiles = cols // TILE
-    cross_out, grad_up, grad_down, grad_bias, grad_in = pl.pallas_call(
+    results = pl.pallas_call(
         functools.partial(kernel, n_dp, n_feat, steps),
         out_shape=(
             jax.ShapeDtypeStruct((part, cols * n_feat), BF16),
@@ -392,6 +420,7 @@
             flops=12 * rows * rank * cols, bytes_accessed=16 * rows * cols, transcendentals=0
         ),
     )(features, cotangent, down_weight.T, up_weight, gate[None, :], bias[None, :])
+    cross_out, grad_up, grad_down, grad_bias, grad_in = placed(*results)
     return cross_out, grad_up, grad_down.T, grad_bias[0], grad_in
 
 

time: 160 us -> 342 us (2.14)
  Pallas kernels: 149 us -> 341 us
  local copies, waits for them, and re-layouts: 7.07 us -> 0 us
    pallas_call x0 -> x1, Pallas kernels: none -> 192 us  [placed(): pl.pallas_call(hand_over, out_shape=tuple((jax.ShapeDtypeStruct(v.shape,...]
    unnamed x13 -> x0, local copies, waits for them, and re-layouts: 7.07 us -> none
where the time goes in v3:
time: 342 us
  Pallas kernels  341 us (100%)
    pallas_call x1, Pallas kernels, placed(): pl.pallas_call(hand_over, out_shape=tuple((jax.ShapeDtypeStruct(v.shape,...  192 us
    pallas_call x1, Pallas kernels, kernel_form(): pl.pallas_call(functools.partial(kernel, n_dp, n_feat, steps), out_shape=...  149 us

profile of v3, /device:TPU:24, one launch (start us, length us, event | category | flops | bytes accessed | tf_op | source)
XLA Modules:
  0.0 341.6 jit_solution(3022580751859345902)
XLA Ops:
  0.6 148.6 %shard_map.101 = (bf16[64,16384]{1,0:T(8,128)(2,1)}, f32[64,4096]{1,0:T(8,128)}, f32[64,4096]{1,0:T(8,128)}, f32[1,4096]{1,0:T(1,128)}, bf16[256,4096]{1,0:T(8,128)(2,1)}) custom-call(bf16[256,4096]{1,0:T(8,128)(2,1)} %x.1, bf16[64,16384]{1,0:T(8,128)(2,1)} %cot.1, bf16[64,4096]{1,0:T(8,128)(2,1)} %bitcast.6, bf16[64,4096]{1,0:T(8,128)(2,1)} %up.1, ...), custom_call_target="tpu_custom_call" | custom-call | flops 6442450944 | bytes 16777216 | tf_op jit(solution)/shard_map/pallas_call | solution.py:372
  149.3 192.4 %shard_map.102 = (bf16[64,16384]{1,0:T(8,128)(2,1)}, f32[64,4096]{1,0:T(8,128)}, f32[64,4096]{1,0:T(8,128)}, f32[1,4096]{1,0:T(1,128)}, bf16[256,4096]{1,0:T(8,128)(2,1)}) custom-call(bf16[64,16384]{1,0:T(8,128)(2,1)} %get-tuple-element.15.refs_0_, f32[64,4096]{1,0:T(8,128)} %get-tuple-element.16.refs_1_, f32[64,4096]{1,0:T(8,128)} %get-tuple-element.17.refs_2_, ...), custom_call_target="tpu_custom_call" | custom-call | tf_op jit(solution)/shard_map/pallas_call | solution.py:351

commit v4 on v3

--- a/solution.py
+++ b/solution.py
@@ -58,7 +58,7 @@
     n_dp, n_feat, steps,
     x, cot, down, up, gate, bias,
     cross_out, grad_up, grad_down, grad_bias, grad_in,
-    cot_v, d_full, u_full, one_scale, cross,
+    cot_own, cot_v, d_full, u_full, one_scale, cross,
     low_t, acc_up, acc_down, out_up, out_down, in_up, in_down,
     gate_v, h_part, h_send, h_in, low, g_part, g_send, g_in, low_grad,
     b_part, b_in,
@@ -114,7 +114,7 @@
     def cot_copy(t, k, f):
         there = pl.ds(pl.multiple_of(f * cols + t * TILE, TILE), TILE)
         return pltpu.make_async_remote_copy(
-            src_ref=cot.at[:, there], dst_ref=cot_v.at[rows_of(mf), tile_at(t)],
+            src_ref=cot_own.at[:, there], dst_ref=cot_v.at[rows_of(mf), tile_at(t)],
             send_sem=cot_s.at[t, k], recv_sem=cot_r.at[t, k],
             device_id=(me, f), device_id_type=MESH,
         )
@@ -141,7 +141,7 @@
     own = [
         move(down, d_full.at[slots(0, 1), :], local.at[0]),
         move(up, u_full.at[slots(0, 1), :], local.at[1]),
-        move(cot.at[:, cols_of(mf)], cot_v.at[rows_of(mf), :], local.at[2]),
+        move(cot, cot_own, local.at[2]),
     ]
     gate_v[...] = jnp.broadcast_to(gate[...], (128, rows)).T
     pl.semaphore_wait(barrier, steps + n_feat - 1)
@@ -156,11 +156,10 @@
 
     early = [None, None]
 
-    def first_hop(w, src, full):
-        return send(src, full.at[slots(1, 2), :], ag_s.at[w, 0], ag_r.at[w, 0], peers[0], mf)
+    def first_hop(w, full):
+        return swap(w, full, 0, 0, 1, 1, 0)
 
     def middle_hops(w, full, hop):
-        own[w].wait()
         for s in range(1, steps - 1):
             hop.wait_recv()
             hop = swap(w, full, s, 0, 2 ** s, 2 ** s, s)
@@ -205,21 +204,25 @@
         started[:] = [other for other in started if other is not copy]
         b_part[...] += b_in[s]
 
-    hop = first_hop(0, down, d_full)
-    start_chunks(cot_copy, 0, tiles * 3 // 4)
+    own[0].wait()
+    hop = first_hop(0, d_full)
+    own[2].wait()
+    start_chunks(cot_copy, 0, tiles // 2)
     hop = middle_hops(0, d_full, hop)
     late = last_hop(0, d_full, hop)
-    hop = first_hop(1, up, u_full)
+    own[1].wait()
+    hop = first_hop(1, u_full)
+    cot_v[rows_of(mf), :] = cot_own[:, cols_of(mf)]
     near, far = slots(0, mid), slots(mid, 2 * mid)
     h_part[:, near] = lax.dot_general(x[...], d_full[near, :], NT, preferred_element_type=F32)
     early[0].wait_recv()
     late.wait_recv()
     h_part[:, far] = lax.dot_general(x[...], d_full[far, :], NT, preferred_element_type=F32)
     parts = spread_parts(0, h_part, h_send, h_in)
-    start_chunks(cot_copy, tiles * 3 // 4, tiles * 7 // 8)
+    start_chunks(cot_copy, tiles // 2, tiles * 5 // 8)
     hop = middle_hops(1, u_full, hop)
     shares = share_sum(0, h_part, h_in, parts, low)
-    start_chunks(cot_copy, tiles * 7 // 8, tiles)
+    start_chunks(cot_copy, tiles * 5 // 8, tiles)
     late = last_hop(1, u_full, hop)
     wait_all(shares)
     early[1].wait_recv()
@@ -233,10 +236,9 @@
         one_scale[:, c] = plus
         cross[:, c] = (x[:, c].astype(F32) * plus).astype(BF16)
 
-    start_chunks(cross_copy, 0, tiles * 3 // 8)
-    own_cross = move(cross.at[rows_of(mf), :], cross_out.at[:, cols_of(mf)], local.at[3])
-
-    own[2].wait()
+    start_chunks(cross_copy, 0, tiles // 4)
+    cross_out[:, cols_of(mf)] = cross[rows_of(mf), :]
+
     g_part[...] = jnp.zeros_like(g_part)
     low_t[...] = low[...].astype(F32).T.astype(BF16)
 
@@ -254,7 +256,7 @@
         out_up[far, c] = terms[mid * shard :].astype(BF16)
 
     parts = spread_parts(1, g_part, g_send, g_in)
-    start_chunks(cross_copy, tiles * 3 // 8, tiles * 5 // 8)
+    start_chunks(cross_copy, tiles // 4, tiles // 2)
 
     def scatter(w, s, out, arriving):
         return send(
@@ -281,7 +283,7 @@
     up_hop = scatter(0, steps - 1, out_up, in_up)
 
     shares = share_sum(1, g_part, g_in, parts, low_grad)
-    start_chunks(cross_copy, tiles * 5 // 8, tiles)
+    start_chunks(cross_copy, tiles // 2, tiles)
     fold(steps - 1, up_hop, *ups)
     up_hop = scatter(0, steps - 2, out_up, in_up)
     wait_all(shares)
@@ -325,24 +327,28 @@
             cross_copy(t, k, f).wait_send()
             cot_copy(t, k, f).wait_send()
 
-    own_cross.wait()
     for copy in started:
         copy.wait_send()
 
 
 def hand_over(*refs):
-    count = len(refs) // 2
-    sems = refs[-1]
-    copies = []
-    for src, dst in zip(refs[:count], refs[count:-1]):
+    count = (len(refs) - 2) // 3
+    arrive, leave = refs[-2:]
+    inward, outward = [], []
+    for src, dst, held in zip(refs[:count], refs[count : 2 * count], refs[2 * count : -2]):
         rows = src.shape[0]
         pieces = 4 if rows % 64 == 0 else 1
         for n in range(pieces):
             at = pl.ds(n * (rows // pieces), rows // pieces)
-            copy = pltpu.make_async_copy(src.at[at, :], dst.at[at, :], sems.at[len(copies)])
-            copy.start()
-            copies.append(copy)
-    for copy in copies:
+            k = len(inward)
+            inward.append(pltpu.make_async_copy(src.at[at, :], held.at[at, :], arrive.at[k]))
+            outward.append(pltpu.make_async_copy(held.at[at, :], dst.at[at, :], leave.at[k]))
+    for copy in inward:
+        copy.start()
+    for first, second in zip(inward, outward):
+        first.wait()
+        second.start()
+    for copy in outward:
         copy.wait()
 
 
@@ -353,7 +359,8 @@
         out_shape=tuple(jax.ShapeDtypeStruct(v.shape, v.dtype) for v in values),
         in_specs=anywhere,
         out_specs=tuple(anywhere),
-        scratch_shapes=[pltpu.SemaphoreType.DMA((4 * len(values),))],
+        scratch_shapes=[pltpu.VMEM(v.shape, v.dtype) for v in values]
+        + [pltpu.SemaphoreType.DMA((4 * len(values),))] * 2,
         compiler_params=pltpu.CompilerParams(vmem_limit_bytes=62 * 2 ** 20),
     )(*values)
 
@@ -379,8 +386,9 @@
             jax.ShapeDtypeStruct((rows, cols), BF16),
         ),
         in_specs=[vmem, hbm, hbm, hbm, vmem, vmem],
-        out_specs=(hbm, vmem, vmem, vmem, vmem),
+        out_specs=(vmem, vmem, vmem, vmem, vmem),
         scratch_shapes=[
+            pltpu.VMEM((part, cols * n_feat), BF16),
             pltpu.VMEM((rows, cols), BF16),
             pltpu.VMEM((rank, cols), BF16),
             pltpu.VMEM((rank, cols), BF16),
@@ -411,7 +419,7 @@
             dma((tiles, others)), dma((tiles, others)),
             dma((2, steps)), dma((2, steps)),
             dma((steps,)), dma((steps,)),
-            dma((4,)),
+            dma((3,)),
         ],
         compiler_params=pltpu.CompilerParams(
             collective_id=0, has_side_effects=True, vmem_limit_bytes=62 * 2 ** 20

time: 342 us -> 158 us (0.46)
  Pallas kernels: 341 us -> 155 us
    pallas_call x1, Pallas kernels: 192 us -> 5.62 us  [placed(): pl.pallas_call(hand_over, out_shape=tuple((jax.ShapeDtypeStruct(v.shape,...]
where the time goes in v4:
time: 158 us; the launch traced here: 156 us
  Pallas kernels  155 us (98%)
    pallas_call x1, Pallas kernels, kernel_form(): pl.pallas_call(functools.partial(kernel, n_dp, n_feat, steps), out_shape=...  150 us
    pallas_call x1, Pallas kernels, placed(): pl.pallas_call(hand_over, out_shape=tuple((jax.ShapeDtypeStruct(v.shape,...  5.62 us

profile of v4, /device:TPU:24, one launch (start us, length us, event | category | flops | bytes accessed | tf_op | source)
XLA Modules:
  0.0 156.0 jit_solution(4914989770982831227)
XLA Ops:
  0.6 149.7 %shard_map.101 = (bf16[64,16384]{1,0:T(8,128)(2,1)}, f32[64,4096]{1,0:T(8,128)}, f32[64,4096]{1,0:T(8,128)}, f32[1,4096]{1,0:T(1,128)}, bf16[256,4096]{1,0:T(8,128)(2,1)}) custom-call(bf16[256,4096]{1,0:T(8,128)(2,1)} %x.1, bf16[64,16384]{1,0:T(8,128)(2,1)} %cot.1, bf16[64,4096]{1,0:T(8,128)(2,1)} %bitcast.6, bf16[64,4096]{1,0:T(8,128)(2,1)} %up.1, ...), custom_call_target="tpu_custom_call" | custom-call | flops 6442450944 | bytes 16777216 | tf_op jit(solution)/shard_map/pallas_call | solution.py:379
  150.4 5.6 %shard_map.102 = (bf16[64,16384]{1,0:T(8,128)(2,1)}, f32[64,4096]{1,0:T(8,128)}, f32[64,4096]{1,0:T(8,128)}, f32[1,4096]{1,0:T(1,128)}, bf16[256,4096]{1,0:T(8,128)(2,1)}) custom-call(bf16[64,16384]{1,0:T(8,128)(2,1)} %get-tuple-element.15.refs_0_, f32[64,4096]{1,0:T(8,128)} %get-tuple-element.16.refs_1_, f32[64,4096]{1,0:T(8,128)} %get-tuple-element.17.refs_2_, ...), custom_call_target="tpu_custom_call" | custom-call | tf_op jit(solution)/shard_map/pallas_call | solution.py:357

commit v5 on v4

--- a/solution.py
+++ b/solution.py
@@ -258,16 +258,16 @@
     parts = spread_parts(1, g_part, g_send, g_in)
     start_chunks(cross_copy, tiles // 4, tiles // 2)
 
-    def scatter(w, s, out, arriving):
+    def scatter(w, s, out, arriving, lo, hi):
+        block = (slots(2 ** s, 2 ** (s + 1)), pl.ds(lo * TILE, (hi - lo) * TILE))
         return send(
-            out.at[slots(2 ** s, 2 ** (s + 1)), :], arriving.at[slots(2 ** s, 2 ** (s + 1)), :],
-            rs_s.at[w, s], rs_r.at[w, s], peers[s], mf)
-
-    def fold(s, copy, acc, out, arriving, result):
+            out.at[block], arriving.at[block], rs_s.at[w, s], rs_r.at[w, s], peers[s], mf)
+
+    def fold(s, copy, lo, hi, acc, out, arriving, result):
         copy.wait_recv()
         n = 2 ** s
 
-        @pl.loop(0, tiles)
+        @pl.loop(lo, hi)
         def _(t):
             c = tile_at(t)
             total = acc[slots(0, n), c] + arriving[slots(n, 2 * n), c].astype(F32)
@@ -280,27 +280,37 @@
     ups = (acc_up, out_up, in_up, grad_up)
     downs = (acc_down, out_down, in_down, grad_down)
     bias_hop = bias_send(steps - 1)
-    up_hop = scatter(0, steps - 1, out_up, in_up)
+    up_hop = scatter(0, steps - 1, out_up, in_up, 0, tiles)
 
     shares = share_sum(1, g_part, g_in, parts, low_grad)
     start_chunks(cross_copy, tiles // 2, tiles)
-    fold(steps - 1, up_hop, *ups)
-    up_hop = scatter(0, steps - 2, out_up, in_up)
+    fold(steps - 1, up_hop, 0, tiles, *ups)
+    up_hop = scatter(0, steps - 2, out_up, in_up, 0, tiles)
     wait_all(shares)
     low_t[...] = low_grad[...].astype(F32).T.astype(BF16)
 
-    @pl.loop(0, tiles)
-    def _(t):
-        c = tile_at(t)
-        terms = jnp.dot(low_t[...], x[:, c], preferred_element_type=F32)
-        acc_down[:, c] = terms[: mid * shard]
-        out_down[far, c] = terms[mid * shard :].astype(BF16)
-
-    down_hop = scatter(1, steps - 1, out_down, in_down)
+    halves = ((1, 0, tiles // 2), (2, tiles // 2, tiles))
+    down_hops = {}
+    for w, lo, hi in halves:
+
+        @pl.loop(lo, hi)
+        def _(t):
+            c = tile_at(t)
+            terms = jnp.dot(low_t[...], x[:, c], preferred_element_type=F32)
+            acc_down[:, c] = terms[: mid * shard]
+            out_down[far, c] = terms[mid * shard :].astype(BF16)
+
+        down_hops[w] = scatter(w, steps - 1, out_down, in_down, lo, hi)
+
+    def down_step(s):
+        for w, lo, hi in halves:
+            fold(s, down_hops[w], lo, hi, *downs)
+            if s:
+                down_hops[w] = scatter(w, s - 1, out_down, in_down, lo, hi)
+
+    down_step(steps - 1)
     bias_fold(steps - 1, bias_hop)
     bias_hop = bias_send(steps - 2)
-    fold(steps - 1, down_hop, *downs)
-    down_hop = scatter(1, steps - 2, out_down, in_down)
 
     @pl.loop(0, tiles)
     def _(t):
@@ -309,12 +319,10 @@
         grad_in[:, c] = (cot_v[:, c].astype(F32) * one_scale[:, c] + back).astype(BF16)
 
     for s in range(steps - 2, -1, -1):
-        fold(s, up_hop, *ups)
+        fold(s, up_hop, 0, tiles, *ups)
         if s:
-            up_hop = scatter(0, s - 1, out_up, in_up)
-        fold(s, down_hop, *downs)
-        if s:
-            down_hop = scatter(1, s - 1, out_down, in_down)
+            up_hop = scatter(0, s - 1, out_up, in_up, 0, tiles)
+        down_step(s)
         bias_fold(s, bias_hop)
         if s:
             bias_hop = bias_send(s - 1)
@@ -417,7 +425,7 @@
             dma((2, others)), dma((2, others)),
             dma((2, others)), dma((2, others)),
             dma((tiles, others)), dma((tiles, others)),
-            dma((2, steps)), dma((2, steps)),
+            dma((3, steps)), dma((3, steps)),
             dma((steps,)), dma((steps,)),
             dma((3,)),
         ],

time: 158 us -> 154 us (0.975)
  Pallas kernels: 155 us -> 152 us
    pallas_call x1, Pallas kernels: 150 us -> 147 us  [kernel_form(): pl.pallas_call(functools.partial(kernel, n_dp, n_feat, steps), out_shape=...]
where the time goes in v5:
time: 154 us; the launch traced here: 153 us
  Pallas kernels  152 us (99%)
    pallas_call x1, Pallas kernels, kernel_form(): pl.pallas_call(functools.partial(kernel, n_dp, n_feat, steps), out_shape=...  147 us
    pallas_call x1, Pallas kernels, placed(): pl.pallas_call(hand_over, out_shape=tuple((jax.ShapeDtypeStruct(v.shape,...  5.62 us

profile of v5, /device:TPU:24, one launch (start us, length us, event | category | flops | bytes accessed | tf_op | source)
XLA Modules:
  0.0 152.8 jit_solution(7820601010043260441)
XLA Ops:
  0.6 146.5 %shard_map.101 = (bf16[64,16384]{1,0:T(8,128)(2,1)}, f32[64,4096]{1,0:T(8,128)}, f32[64,4096]{1,0:T(8,128)}, f32[1,4096]{1,0:T(1,128)}, bf16[256,4096]{1,0:T(8,128)(2,1)}) custom-call(bf16[256,4096]{1,0:T(8,128)(2,1)} %x.1, bf16[64,16384]{1,0:T(8,128)(2,1)} %cot.1, bf16[64,4096]{1,0:T(8,128)(2,1)} %bitcast.6, bf16[64,4096]{1,0:T(8,128)(2,1)} %up.1, ...), custom_call_target="tpu_custom_call" | custom-call | flops 6442450944 | bytes 16777216 | tf_op jit(solution)/shard_map/pallas_call | solution.py:387
  147.2 5.6 %shard_map.102 = (bf16[64,16384]{1,0:T(8,128)(2,1)}, f32[64,4096]{1,0:T(8,128)}, f32[64,4096]{1,0:T(8,128)}, f32[1,4096]{1,0:T(1,128)}, bf16[256,4096]{1,0:T(8,128)(2,1)}) custom-call(bf16[64,16384]{1,0:T(8,128)(2,1)} %get-tuple-element.15.refs_0_, f32[64,4096]{1,0:T(8,128)} %get-tuple-element.16.refs_1_, f32[64,4096]{1,0:T(8,128)} %get-tuple-element.17.refs_2_, ...), custom_call_target="tpu_custom_call" | custom-call | tf_op jit(solution)/shard_map/pallas_call | solution.py:365
